TPU v7x, 32 devices: a whole 2x2x4 slice. The times are simulated.
32 devices in a mesh: tm: 16 (over z, y, x), chan: 2 (over core).
Axes of the slice: x: 2, y: 2, z: 4, core: 2. Of those that a mesh axis runs over, the one named last changes fastest.
Arguments:
- field: float32 [2, 2, 64, 16384], P(None, None, 'chan', 'tm'), may hold values from -15.5 to 15.5
- noise: float32 [1, 2, 2, 64, 16384], P(None, None, None, 'chan', 'tm'), may hold values from -1.25 to 1.25
- assign: int32 [64], P('chan'), may hold values from 0 to 63, each once
Outputs:
- received: float32 [2, 2, 64, 16384], P(None, None, 'chan', 'tm')
- recovered: float32 [2, 2, 64, 16384], P(None, None, 'chan', 'tm')
All inputs are finite; a program needn't handle non-finite values.
Results may differ from a plain program's by a relative error of at most 0.0003.
Values sent between devices are 32-bit elements; how exact they have to be, the bound alone decides.
A program may use at most 64 MiB of HBM per device.

v0:
```python
import jax
import jax.numpy as jnp
from jax import lax
from jax.sharding import PartitionSpec as P

OPTICAL_CHANNELS = 64
FILTER_HALF_TAPS = 128
STEPS = 2
FIBER_SECTIONS = 1


ATT = 0.955
GAMMA = 0.004
WALK = 0.5
SPREAD = 0.4
CHIRP = 0.25
EPS = 1e-06


def padded(array, sides, width):
    for axis, dim in sides:
        count, length = (lax.axis_size(axis), array.shape[dim])
        up = [(i, (i + 1) % count) for i in range(count)]
        down = [(j, i) for i, j in up]
        last = lax.slice_in_dim(array, length - width, length, axis=dim)
        leading = lax.slice_in_dim(array, 0, width, axis=dim)
        before = lax.ppermute(last, axis, up)
        after = lax.ppermute(leading, axis, down)
        array = jnp.concatenate([before, array, after], axis=dim)
    return array


def tap_tables(channel_ids, sign, reach, channels):
    rows = jnp.arange(3 * reach, dtype=jnp.int32)[:, None]
    cols = jnp.arange(reach, dtype=jnp.int32)[None, :]
    lag = cols - rows + reach
    interior_part = (jnp.abs(lag) <= reach).astype(jnp.float32)
    centre = (
        WALK * reach * (2.0 * channel_ids.astype(jnp.float32) - (channels - 1)) / (channels - 1)
    )
    centre = centre[:, None, None]
    width = SPREAD * reach
    offset = sign * lag.astype(jnp.float32)[None] - centre
    symbol_profile = jnp.exp(-jnp.square(offset / width))
    turn = jnp.square(offset) / (2.0 * CHIRP * reach)
    taps = jnp.arange(-reach, reach + 1, dtype=jnp.int32).astype(jnp.float32)
    scale = jnp.sqrt(
        jnp.sum(jnp.exp(-2.0 * jnp.square((taps[None, :] - centre[:, :, 0]) / width)), axis=1)
    )
    scale = scale[:, None, None]
    mat_re = interior_part * symbol_profile * jnp.cos(turn) / scale
    mat_im = sign * interior_part * symbol_profile * jnp.sin(turn) / scale
    return (mat_re, mat_im)


def disperse(ext, mat_re, mat_im, reach):
    pols, parts, chans, segment_length = ext.shape
    blocks = segment_length // reach - 2
    rows = ext.reshape(pols, parts, chans, blocks + 2, reach)
    window = jnp.concatenate(
        [rows[:, :, :, 0:blocks], rows[:, :, :, 1 : blocks + 1], rows[:, :, :, 2 : blocks + 2]],
        axis=4,
    )
    real = window[:, 0]
    imag = window[:, 1]
    high = lax.Precision.HIGHEST
    out_re = jnp.einsum("pcjq,cqn->pcjn", real, mat_re, precision=high) - jnp.einsum(
        "pcjq,cqn->pcjn", imag, mat_im, precision=high
    )
    out_im = jnp.einsum("pcjq,cqn->pcjn", real, mat_im, precision=high) + jnp.einsum(
        "pcjq,cqn->pcjn", imag, mat_re, precision=high
    )
    return jnp.stack([out_re, out_im], axis=1).reshape(pols, parts, chans, blocks * reach)


def rotate(ext, sign, own, total):
    angle = sign * GAMMA * (2.0 * total[None, :] - own)
    cosine = jnp.cos(angle)
    sine = jnp.sin(angle)
    real = ext[:, 0]
    imag = ext[:, 1]
    return jnp.stack([real * cosine - imag * sine, real * sine + imag * cosine], axis=1)


def on_device(field, noise, assign):
    forward = tap_tables(assign, 1.0, FILTER_HALF_TAPS, OPTICAL_CHANNELS)
    backward = tap_tables(assign, -1.0, FILTER_HALF_TAPS, OPTICAL_CHANNELS)
    total_len = lax.axis_size("tm") * field.shape[3]
    depth = 1
    counts = [min(depth, STEPS - start) for start in range(0, STEPS, depth)]

    def widen(current, count):
        return padded(current, (("tm", 3),), count * FILTER_HALF_TAPS)

    def nonlinear(ext, sign):
        own = jnp.sum(jnp.square(ext), axis=(0, 1))
        total = lax.psum(jnp.sum(own, axis=0), "chan")
        return rotate(ext, sign, own, total)

    current = field
    forward_current = current
    for count in counts:
        ext = widen(forward_current, count)
        ext = disperse(ext, forward[0], forward[1], FILTER_HALF_TAPS) * ATT
        ext = nonlinear(ext, 1.0)
        forward_current = ext
    current = forward_current
    last_noise = noise[FIBER_SECTIONS - 1]
    field_sq = jnp.sum(jnp.square(current), axis=(0, 1, 3))
    cross = jnp.sum(current * last_noise, axis=(0, 1, 3))
    noise_sq = jnp.sum(jnp.square(last_noise), axis=(0, 1, 3))
    field_sq, cross, noise_sq = lax.psum((field_sq, cross, noise_sq), "tm")
    gain = lax.rsqrt(field_sq / total_len + EPS)
    received = current * gain[None, None, :, None] + last_noise
    arrival = (gain * gain * field_sq + 2.0 * gain * cross + noise_sq) / total_len
    current = received
    rescale = jnp.sqrt(ATT ** (2 * STEPS) / (arrival + EPS))
    current = current * rescale[None, None, :, None]
    backward_current = current
    for count in counts:
        ext = widen(backward_current, count)
        ext = nonlinear(ext, -1.0) / ATT
        ext = disperse(ext, backward[0], backward[1], FILTER_HALF_TAPS)
        backward_current = ext
    current = backward_current
    return (received, current)


def solution(mesh):
    placed = (P(None, None, "chan", "tm"), P(None, None, None, "chan", "tm"), P("chan"))
    return jax.shard_map(
        on_device,
        mesh=mesh,
        in_specs=placed,
        out_specs=(P(None, None, "chan", "tm"), P(None, None, "chan", "tm")),
        check_vma=False,
    )
```

profile of v0, /device:TPU:0, one launch (start us, length us, event | category | flops | bytes accessed | tf_op | source)
XLA Modules:
  0.0 530.7 jit_solution(8636539628690278218)
XLA Ops:
  0.6 0.9 fusion.256
  1.5 3.0 collective-permute-start
  4.5 4.1 collective-permute-start.1
  8.6 0.7 add_multiply_fusion
  9.3 0.2 exponential_reduce_fusion
  9.5 1.3 collective-permute-done
  10.8 1.1 pad_maximum_fusion.6
  11.9 0.1 reshape.243
  12.0 0.1 fusion.253
  12.1 0.1 pad_maximum_fusion
  12.3 0.1 fusion.249
  12.4 26.7 %fusion.19 = f32[32,128,2,8]{1,3,2,0:T(8,128)S(1)} fusion(f32[32]{0:T(128)S(1)} %sqrt.11, f32[32]{0:T(128)S(1)} %add_multiply_fusion, f32[384,128]{1,0:T(8,128)S(1)} %fusion.205, f32[384,128]{1,0:T(8,128)S(1)} %fusion.215, f32[2,1,32,8,384]{4,3,2,1,0:T(8,128)S(1)} %get-tuple-element.20), kind=kOutput, calls=%fused_computation.20 | convolution fusion | flops 316145664 | bytes 1442048 | tf_op jit(solution)/shard_map/pcjq,cqn->pcjn/dot_general | solution.py:67
  39.0 27.0 %fusion.17 = f32[32,128,2,8]{1,3,2,0:T(8,128)S(1)} fusion(f32[32]{0:T(128)S(1)} %sqrt.11, f32[32]{0:T(128)S(1)} %add_multiply_fusion, f32[384,128]{1,0:T(8,128)S(1)} %fusion.205, f32[384,128]{1,0:T(8,128)S(1)} %fusion.215, f32[2,1,32,8,384]{4,3,2,1,0:T(8,128)S(1)} %get-tuple-element.21), kind=kOutput, calls=%fused_computation.19 | convolution fusion | flops 316145664 | bytes 1442048 | tf_op jit(solution)/shard_map/pcjq,cqn->pcjn/dot_general | solution.py:70
  66.1 27.1 %fusion.182 = f32[2,32,8,128]{3,2,0,1:T(8,128)S(1)} fusion(f32[32,128,2,8]{1,3,2,0:T(8,128)S(1)} %fusion.19, f32[32]{0:T(128)S(1)} %sqrt.11, f32[32]{0:T(128)S(1)} %add_multiply_fusion, f32[384,128]{1,0:T(8,128)S(1)} %fusion.205, f32[384,128]{1,0:T(8,128)S(1)} %fusion.215, f32[2,1,32,8,384]{4,3,2,1,0:T(8,128)S(1)} %get-tuple-element.21), kind=kOutput, calls=%fused_computation.156 | convolution fusion | flops 316211200 | bytes 1704192 | tf_op jit(solution)/shard_map/pcjq,cqn->pcjn/dot_general | solution.py:67
  93.2 27.5 %fusion.188 = f32[2,32,8,128]{3,2,0,1:T(8,128)S(1)} fusion(f32[32,128,2,8]{1,3,2,0:T(8,128)S(1)} %fusion.17, f32[32]{0:T(128)S(1)} %sqrt.11, f32[32]{0:T(128)S(1)} %add_multiply_fusion, f32[384,128]{1,0:T(8,128)S(1)} %fusion.205, f32[384,128]{1,0:T(8,128)S(1)} %fusion.215, f32[2,1,32,8,384]{4,3,2,1,0:T(8,128)S(1)} %get-tuple-element.20), kind=kOutput, calls=%fused_computation.158 | convolution fusion | flops 316211200 | bytes 1704192 | tf_op jit(solution)/shard_map/pcjq,cqn->pcjn/dot_general | solution.py:70
  120.7 0.1 stack.65
  120.9 0.1 stack.64
  121.3 2.5 psum.49
  123.7 0.5 fusion.211
  124.3 0.4 collective-permute-start.2
  124.7 5.3 %collective-permute-start.3 = (f32[2,2,32,128]{3,2,1,0:T(8,128)S(1)}, f32[2,2,32,128]{3,2,1,0:T(8,128)S(1)}, u32[]{:S(2)}, u32[]{:S(2)}) collective-permute-start(f32[2,2,32,128]{3,2,1,0:T(8,128)S(1)} %get-tuple-element.50), channel_id=1, source_target_pairs={{2,0},{4,2},{6,4},{8,6},{10,8},{12,10},{14,12},{16,14},{18,16},{20... | collective-permute-start | bytes 196616 | tf_op jit(solution)/shard_map/ppermute | solution.py:28
  130.1 2.4 collective-permute-done.2
  132.5 0.1 reshape.244
  132.6 0.1 fusion.252
  132.7 0.1 pad_maximum_fusion.1
  132.8 0.1 fusion.248
  132.9 26.7 %fusion.15 = f32[32,128,2,8]{1,3,2,0:T(8,128)S(1)} fusion(f32[32]{0:T(128)S(1)} %sqrt.11, f32[32]{0:T(128)S(1)} %add_multiply_fusion, f32[384,128]{1,0:T(8,128)S(1)} %fusion.205, f32[384,128]{1,0:T(8,128)S(1)} %fusion.215, f32[2,1,32,8,384]{4,3,2,1,0:T(8,128)S(1)} %get-tuple-element.18), kind=kOutput, calls=%fused_computation.18 | convolution fusion | flops 316145664 | bytes 1442048 | tf_op jit(solution)/shard_map/pcjq,cqn->pcjn/dot_general | solution.py:67
  159.6 27.1 %fusion.13 = f32[32,128,2,8]{1,3,2,0:T(8,128)S(1)} fusion(f32[32]{0:T(128)S(1)} %sqrt.11, f32[32]{0:T(128)S(1)} %add_multiply_fusion, f32[384,128]{1,0:T(8,128)S(1)} %fusion.205, f32[384,128]{1,0:T(8,128)S(1)} %fusion.215, f32[2,1,32,8,384]{4,3,2,1,0:T(8,128)S(1)} %get-tuple-element.19), kind=kOutput, calls=%fused_computation.17 | convolution fusion | flops 316145664 | bytes 1442048 | tf_op jit(solution)/shard_map/pcjq,cqn->pcjn/dot_general | solution.py:70
  186.7 27.1 %fusion.194 = f32[2,32,8,128]{3,2,0,1:T(8,128)S(1)} fusion(f32[32,128,2,8]{1,3,2,0:T(8,128)S(1)} %fusion.15, f32[32]{0:T(128)S(1)} %sqrt.11, f32[32]{0:T(128)S(1)} %add_multiply_fusion, f32[384,128]{1,0:T(8,128)S(1)} %fusion.205, f32[384,128]{1,0:T(8,128)S(1)} %fusion.215, f32[2,1,32,8,384]{4,3,2,1,0:T(8,128)S(1)} %get-tuple-element.19), kind=kOutput, calls=%fused_computation.160 | convolution fusion | flops 316211200 | bytes 1704192 | tf_op jit(solution)/shard_map/pcjq,cqn->pcjn/dot_general | solution.py:67
  213.8 27.5 %fusion.200 = f32[2,32,8,128]{3,2,0,1:T(8,128)S(1)} fusion(f32[32,128,2,8]{1,3,2,0:T(8,128)S(1)} %fusion.13, f32[32]{0:T(128)S(1)} %sqrt.11, f32[32]{0:T(128)S(1)} %add_multiply_fusion, f32[384,128]{1,0:T(8,128)S(1)} %fusion.205, f32[384,128]{1,0:T(8,128)S(1)} %fusion.215, f32[2,1,32,8,384]{4,3,2,1,0:T(8,128)S(1)} %get-tuple-element.18), kind=kOutput, calls=%fused_computation.162 | convolution fusion | flops 316211200 | bytes 1704192 | tf_op jit(solution)/shard_map/pcjq,cqn->pcjn/dot_general | solution.py:70
  241.3 0.1 stack.69
  241.6 0.1 stack.68
  241.9 2.6 psum.50
  244.5 0.5 fusion.213
  245.1 0.2 fusion.203
  245.3 42.1 %all-reduce = (f32[32]{0:T(128)S(1)}, f32[32]{0:T(128)S(1)}, f32[32]{0:T(128)S(1)}) all-reduce(f32[32]{0:T(128)S(1)} %get-tuple-element.7, f32[32]{0:T(128)S(1)} %get-tuple-element.8, f32[32]{0:T(128)S(1)} %get-tuple-element.6), channel_id=1, replica_groups=mesh['tm'=16,'chan'=2] {'tm'}, use_global_device_ids=true, to_apply=%region_8.0 | all-reduce | flops 96 | bytes 768 | tf_op jit(solution)/shard_map/psum | solution.py:112
  287.4 1.0 broadcast_multiply_fusion
  288.5 5.6 %collective-permute-start.5 = (f32[2,2,32,128]{3,2,1,0:T(8,128)S(1)}, f32[2,2,32,128]{3,2,1,0:T(8,128)S(1)}, u32[]{:S(2)}, u32[]{:S(2)}) collective-permute-start(f32[2,2,32,128]{3,2,1,0:T(8,128)S(1)} %get-tuple-element.47), channel_id=1, source_target_pairs={{2,0},{4,2},{6,4},{8,6},{10,8},{12,10},{14,12},{16,14},{18,16},{20... | collective-permute-start | bytes 196616 | tf_op jit(solution)/shard_map/ppermute | solution.py:28
  294.2 2.2 collective-permute-done.4
  296.4 2.5 psum.54
  299.0 0.6 fusion.207
  299.8 0.1 copy_multiply_fusion.1
  299.9 0.1 fusion.251
  300.1 0.1 pad_maximum_fusion.2
  300.2 26.7 %fusion.47 = f32[32,128,2,8]{1,3,2,0:T(8,128)S(1)} fusion(f32[384,128]{1,0:T(8,128)S(1)} %get-tuple-element.65, f32[32]{0:T(128)S(1)} %sqrt.11, f32[32]{0:T(128)S(1)} %add_multiply_fusion, f32[384,128]{1,0:T(8,128)S(1)} %fusion.215, f32[2,2,32,8,384]{4,3,0,2,1:T(8,128)S(1)} %pad_maximum_fusion.2), kind=kOutput, calls=%fused_computation.41 | convolution fusion | flops 316145664 | bytes 1442816 | tf_op jit(solution)/shard_map/pcjq,cqn->pcjn/dot_general | solution.py:70
  326.8 27.1 %fusion.49 = f32[32,128,2,8]{1,3,2,0:T(8,128)S(1)} fusion(f32[384,128]{1,0:T(8,128)S(1)} %get-tuple-element.65, f32[32]{0:T(128)S(1)} %sqrt.11, f32[32]{0:T(128)S(1)} %add_multiply_fusion, f32[384,128]{1,0:T(8,128)S(1)} %fusion.215, f32[2,2,32,8,384]{4,3,0,2,1:T(8,128)S(1)} %pad_maximum_fusion.2), kind=kOutput, calls=%fused_computation.42 | convolution fusion | flops 316145664 | bytes 1442816 | tf_op jit(solution)/shard_map/pcjq,cqn->pcjn/dot_general | solution.py:67
  354.0 27.1 %fusion.164 = f32[2,32,8,128]{3,2,0,1:T(8,128)S(1)} fusion(f32[32,128,2,8]{1,3,2,0:T(8,128)S(1)} %fusion.47, f32[384,128]{1,0:T(8,128)S(1)} %get-tuple-element.64, f32[384,128]{1,0:T(8,128)S(1)} %get-tuple-element.65, f32[32]{0:T(128)S(1)} %sqrt.11, f32[32]{0:T(128)S(1)} %add_multiply_fusion, f32[2,2,32,8,384]{4,3,0,2,1:T(8,128)S(1)} %pad_maximum_fusion.2), kind=kOutput, calls=%fused_computation.150 | convolution fusion | flops 316211200 | bytes 1704960 | tf_op jit(solution)/shard_map/pcjq,cqn->pcjn/dot_general | solution.py:70
  381.1 0.1 stack.76
  381.2 27.5 %fusion.158 = f32[2,32,8,128]{3,2,0,1:T(8,128)S(1)} fusion(f32[32,128,2,8]{1,3,2,0:T(8,128)S(1)} %fusion.49, f32[384,128]{1,0:T(8,128)S(1)} %get-tuple-element.64, f32[384,128]{1,0:T(8,128)S(1)} %get-tuple-element.65, f32[32]{0:T(128)S(1)} %sqrt.11, f32[32]{0:T(128)S(1)} %add_multiply_fusion, f32[2,2,32,8,384]{4,3,0,2,1:T(8,128)S(1)} %pad_maximum_fusion.2), kind=kOutput, calls=%fused_computation.148 | convolution fusion | flops 316211200 | bytes 1704960 | tf_op jit(solution)/shard_map/pcjq,cqn->pcjn/dot_general | solution.py:67
  408.7 0.1 stack.75
  409.1 5.7 %collective-permute-start.7 = (f32[2,2,32,128]{3,2,0,1:T(8,128)S(1)}, f32[2,2,32,128]{3,2,0,1:T(8,128)S(1)}, u32[]{:S(2)}, u32[]{:S(2)}) collective-permute-start(f32[2,2,32,128]{3,2,0,1:T(8,128)S(1)} %get-tuple-element.45), channel_id=1, source_target_pairs={{2,0},{4,2},{6,4},{8,6},{10,8},{12,10},{14,12},{16,14},{18,16},{20... | collective-permute-start | bytes 196616 | tf_op jit(solution)/shard_map/ppermute | solution.py:28
  414.8 2.4 collective-permute-done.6
  417.3 2.5 psum.55
  419.8 0.6 fusion.209
  420.6 0.1 copy_multiply_fusion
  420.7 0.1 fusion.250
  420.9 0.1 pad_maximum_fusion.3
  421.0 26.7 %fusion.43 = f32[32,128,2,8]{1,3,2,0:T(8,128)S(1)} fusion(f32[384,128]{1,0:T(8,128)S(1)} %get-tuple-element.65, f32[32]{0:T(128)S(1)} %sqrt.11, f32[32]{0:T(128)S(1)} %add_multiply_fusion, f32[384,128]{1,0:T(8,128)S(1)} %fusion.215, f32[2,2,32,8,384]{4,3,0,2,1:T(8,128)S(1)} %pad_maximum_fusion.3), kind=kOutput, calls=%fused_computation.39 | convolution fusion | flops 316145664 | bytes 1442816 | tf_op jit(solution)/shard_map/pcjq,cqn->pcjn/dot_general | solution.py:70
  447.7 27.1 %fusion.45 = f32[32,128,2,8]{1,3,2,0:T(8,128)S(1)} fusion(f32[384,128]{1,0:T(8,128)S(1)} %get-tuple-element.65, f32[32]{0:T(128)S(1)} %sqrt.11, f32[32]{0:T(128)S(1)} %add_multiply_fusion, f32[384,128]{1,0:T(8,128)S(1)} %fusion.215, f32[2,2,32,8,384]{4,3,0,2,1:T(8,128)S(1)} %pad_maximum_fusion.3), kind=kOutput, calls=%fused_computation.40 | convolution fusion | flops 316145664 | bytes 1442816 | tf_op jit(solution)/shard_map/pcjq,cqn->pcjn/dot_general | solution.py:67
  474.8 27.1 %fusion.176 = f32[2,32,8,128]{3,2,0,1:T(8,128)S(1)} fusion(f32[32,128,2,8]{1,3,2,0:T(8,128)S(1)} %fusion.43, f32[384,128]{1,0:T(8,128)S(1)} %get-tuple-element.64, f32[384,128]{1,0:T(8,128)S(1)} %get-tuple-element.65, f32[32]{0:T(128)S(1)} %sqrt.11, f32[32]{0:T(128)S(1)} %add_multiply_fusion, f32[2,2,32,8,384]{4,3,0,2,1:T(8,128)S(1)} %pad_maximum_fusion.3), kind=kOutput, calls=%fused_computation.154 | convolution fusion | flops 316211200 | bytes 1704960 | tf_op jit(solution)/shard_map/pcjq,cqn->pcjn/dot_general | solution.py:70
  501.9 0.1 stack.82
  502.2 27.1 %fusion.170 = f32[2,32,8,128]{3,2,0,1:T(8,128)S(1)} fusion(f32[32,128,2,8]{1,3,2,0:T(8,128)S(1)} %fusion.45, f32[384,128]{1,0:T(8,128)S(1)} %get-tuple-element.64, f32[384,128]{1,0:T(8,128)S(1)} %get-tuple-element.65, f32[32]{0:T(128)S(1)} %sqrt.11, f32[32]{0:T(128)S(1)} %add_multiply_fusion, f32[2,2,32,8,384]{4,3,0,2,1:T(8,128)S(1)} %pad_maximum_fusion.3), kind=kOutput, calls=%fused_computation.152 | convolution fusion | flops 316211200 | bytes 1704960 | tf_op jit(solution)/shard_map/pcjq,cqn->pcjn/dot_general | solution.py:67
  529.3 0.1 stack.81
  529.5 0.8 pad_maximum_fusion.11
  (42 shorter events, 2.0 us)
Async XLA Ops:
  1.5 9.3 %collective-permute-start = (f32[2,2,32,128]{3,2,1,0:T(8,128)S(1)}, f32[2,2,32,128]{3,2,1,0:T(8,128)S(1)}, u32[]{:S(2)}, u32[]{:S(2)}) collective-permute-start(f32[2,2,32,128]{3,2,1,0:T(8,128)S(1)} %get-tuple-element.52), channel_id=1, source_target_pairs={{0,2},{2,4},{4,6},{6,8},{8,10},{10,12},{12,14},{14,16},{16,18},{18... | collective-permute-start | bytes 196616 | tf_op jit(solution)/shard_map/ppermute | solution.py:27
  4.5 6.3 %collective-permute-start.1 = (f32[2,2,32,128]{3,2,1,0:T(8,128)S(1)}, f32[2,2,32,128]{3,2,1,0:T(8,128)S(1)}, u32[]{:S(2)}, u32[]{:S(2)}) collective-permute-start(f32[2,2,32,128]{3,2,1,0:T(8,128)S(1)} %get-tuple-element.53), channel_id=1, source_target_pairs={{2,0},{4,2},{6,4},{8,6},{10,8},{12,10},{14,12},{16,14},{18,16},{20... | collective-permute-start | bytes 196616 | tf_op jit(solution)/shard_map/ppermute | solution.py:28
  124.3 8.1 %collective-permute-start.2 = (f32[2,2,32,128]{3,2,1,0:T(8,128)S(1)}, f32[2,2,32,128]{3,2,1,0:T(8,128)S(1)}, u32[]{:S(2)}, u32[]{:S(2)}) collective-permute-start(f32[2,2,32,128]{3,2,1,0:T(8,128)S(1)} %get-tuple-element.49), channel_id=1, source_target_pairs={{0,2},{2,4},{4,6},{6,8},{8,10},{10,12},{12,14},{14,16},{16,18},{18... | collective-permute-start | bytes 196616 | tf_op jit(solution)/shard_map/ppermute | solution.py:27
  124.7 7.7 %collective-permute-start.3 = (f32[2,2,32,128]{3,2,1,0:T(8,128)S(1)}, f32[2,2,32,128]{3,2,1,0:T(8,128)S(1)}, u32[]{:S(2)}, u32[]{:S(2)}) collective-permute-start(f32[2,2,32,128]{3,2,1,0:T(8,128)S(1)} %get-tuple-element.50), channel_id=1, source_target_pairs={{2,0},{4,2},{6,4},{8,6},{10,8},{12,10},{14,12},{16,14},{18,16},{20... | collective-permute-start | bytes 196616 | tf_op jit(solution)/shard_map/ppermute | solution.py:28
  241.8 3.3 copy-start
  288.4 7.9 %collective-permute-start.4 = (f32[2,2,32,128]{3,2,1,0:T(8,128)S(1)}, f32[2,2,32,128]{3,2,1,0:T(8,128)S(1)}, u32[]{:S(2)}, u32[]{:S(2)}) collective-permute-start(f32[2,2,32,128]{3,2,1,0:T(8,128)S(1)} %get-tuple-element.46), channel_id=1, source_target_pairs={{0,2},{2,4},{4,6},{6,8},{8,10},{10,12},{12,14},{14,16},{16,18},{18... | collective-permute-start | bytes 196616 | tf_op jit(solution)/shard_map/ppermute | solution.py:27
  288.5 7.9 %collective-permute-start.5 = (f32[2,2,32,128]{3,2,1,0:T(8,128)S(1)}, f32[2,2,32,128]{3,2,1,0:T(8,128)S(1)}, u32[]{:S(2)}, u32[]{:S(2)}) collective-permute-start(f32[2,2,32,128]{3,2,1,0:T(8,128)S(1)} %get-tuple-element.47), channel_id=1, source_target_pairs={{2,0},{4,2},{6,4},{8,6},{10,8},{12,10},{14,12},{16,14},{18,16},{20... | collective-permute-start | bytes 196616 | tf_op jit(solution)/shard_map/ppermute | solution.py:28
  409.1 8.1 %collective-permute-start.6 = (f32[2,2,32,128]{3,2,0,1:T(8,128)S(1)}, f32[2,2,32,128]{3,2,0,1:T(8,128)S(1)}, u32[]{:S(2)}, u32[]{:S(2)}) collective-permute-start(f32[2,2,32,128]{3,2,0,1:T(8,128)S(1)} %get-tuple-element.44), channel_id=1, source_target_pairs={{0,2},{2,4},{4,6},{6,8},{8,10},{10,12},{12,14},{14,16},{16,18},{18... | collective-permute-start | bytes 196616 | tf_op jit(solution)/shard_map/ppermute | solution.py:27
  409.1 8.0 %collective-permute-start.7 = (f32[2,2,32,128]{3,2,0,1:T(8,128)S(1)}, f32[2,2,32,128]{3,2,0,1:T(8,128)S(1)}, u32[]{:S(2)}, u32[]{:S(2)}) collective-permute-start(f32[2,2,32,128]{3,2,0,1:T(8,128)S(1)} %get-tuple-element.45), channel_id=1, source_target_pairs={{2,0},{4,2},{6,4},{8,6},{10,8},{12,10},{14,12},{16,14},{18,16},{20... | collective-permute-start | bytes 196616 | tf_op jit(solution)/shard_map/ppermute | solution.py:28
where the time goes:
time: 541 us; the launch traced here: 531 us
  matrix products  433 us (80%)
  blocking collectives  52.1 us (10%)
  starting transfers between devices  24.2 us (4%)
  waiting for transfers between devices  8.18 us (2%)
  other arithmetic  7.78 us (1%)
    dot_general x4, matrix products, disperse(): jnp.einsum('pcjq,cqn->pcjn', real, mat_im, precision=high)  109 us
    dot_general x4, matrix products, disperse(): jnp.einsum('pcjq,cqn->pcjn', imag, mat_im, precision=high)  109 us
    dot_general x4, matrix products, disperse(): jnp.einsum('pcjq,cqn->pcjn', real, mat_re, precision=high)  108 us
    dot_general x4, matrix products, disperse(): jnp.einsum('pcjq,cqn->pcjn', imag, mat_re, precision=high)  107 us
    psum x1, blocking collectives, on_device(): field_sq, cross, noise_sq = lax.psum((field_sq, cross, noise_sq), 'tm')  42.1 us
    ppermute x4, starting transfers between devices, padded(): after = lax.ppermute(leading, axis, down)  20.7 us
  transfers between devices with their start and end apart: 8, of which 4 were waited for; matrix products, arithmetic and copies ran while one was open for 0% of the time, Pallas kernels for 0%

commit v1 on v0

v1 whole, which is shorter than its diff:
```python
import functools
import jax
import jax.numpy as jnp
from jax import lax
from jax.experimental import pallas as pl
from jax.experimental.pallas import tpu as pltpu
from jax.sharding import PartitionSpec as P

OPTICAL_CHANNELS = 64
REACH = 128
STEPS = 2
ATT = 0.955
GAMMA = 0.004
WALK = 0.5
SPREAD = 0.4
CHIRP = 0.25
EPS = 1e-06
GROUP = 8
MESH = pl.DeviceIdType.MESH


def tap_rows(channel_ids):
    lag = jnp.arange(-REACH, 2 * REACH, dtype=jnp.int32)
    centre = (
        WALK * REACH * (2.0 * channel_ids.astype(jnp.float32) - (OPTICAL_CHANNELS - 1))
        / (OPTICAL_CHANNELS - 1)
    )[:, None]
    width = SPREAD * REACH
    taps = jnp.arange(-REACH, REACH + 1, dtype=jnp.int32).astype(jnp.float32)
    scale = jnp.sqrt(
        jnp.sum(jnp.exp(-2.0 * jnp.square((taps[None, :] - centre) / width)), axis=1)
    )[:, None]
    rows, ends = [], []
    for sign, factor in ((1.0, ATT), (-1.0, 1.0 / ATT)):
        offset = sign * lag.astype(jnp.float32)[None] - centre
        profile = factor * jnp.exp(-jnp.square(offset / width)) / scale
        turn = jnp.square(offset) / (2.0 * CHIRP * REACH)
        for part in (profile * jnp.cos(turn), sign * profile * jnp.sin(turn)):
            rows += [part[:, :REACH], part[:, REACH : 2 * REACH]]
            ends.append(jnp.broadcast_to(part[:, 2 * REACH : 2 * REACH + 1], part[:, :REACH].shape))
    rows += ends
    rows += [jnp.zeros_like(rows[0])] * 4
    return jnp.stack(rows, axis=1)


def cos_sin(angle):
    n = jnp.floor(angle * 0.3183098861837907 + 0.5)
    r = ((angle - n * 3.140625) - n * 9.67502593994140625e-4) - n * 1.509957990978376432e-7
    sgn = 1.0 - 2.0 * (n - 2.0 * jnp.floor(0.5 * n))
    z = r * r
    s = -1.0 / 39916800.0
    for k in (1.0 / 362880.0, -1.0 / 5040.0, 1.0 / 120.0, -1.0 / 6.0, 1.0):
        s = s * z + k
    c = 1.0 / 479001600.0
    for k in (-1.0 / 3628800.0, 1.0 / 40320.0, -1.0 / 720.0, 1.0 / 24.0, -0.5, 1.0):
        c = c * z + k
    return c * sgn, s * (r * sgn)


def kernel(
    nt, nc, total_len,
    field_hbm, noise_hbm, x_ref, noise_ref, taps_ref,
    rec_ref, out_ref,
    t_hi, t_lo, y_ref, z_ref, pw_ref, h_ref, e_ref, hr_ref, tsend, trecv, tot_ref, stat, ssend, srecv, gain_ref,
    h_send, h_recv, e_send, e_recv, c_send, c_recv, s_send, s_recv,
):
    slots = x_ref.shape[0]
    length = field_hbm.shape[3]
    groups = slots // GROUP
    tm, ch = lax.axis_index("tm"), lax.axis_index("chan")
    right, left = lax.rem(tm + 1, nt), lax.rem(tm + nt - 1, nt)
    row = lax.broadcasted_iota(jnp.int32, (8, 128), 0)

    barrier = pltpu.get_barrier_semaphore()

    def greet(d, _):
        pl.semaphore_signal(
            barrier, inc=1, device_id={"tm": lax.rem(tm + d, nt)}, device_id_type=MESH
        )
        return 0

    lax.fori_loop(1, nt, greet, 0)
    for d in range(1, nc):
        pl.semaphore_signal(
            barrier, inc=1, device_id={"chan": lax.rem(ch + d, nc)}, device_id_type=MESH
        )
    pl.semaphore_wait(barrier, nt - 1 + nc - 1)

    def first_edge(k, side):
        source = (field_hbm, noise_hbm)[k]
        start = length - REACH if side == 0 else 0
        return pltpu.make_async_remote_copy(
            src_ref=source.at[:, :, :, pl.ds(start, REACH)],
            dst_ref=h_ref.at[k, side],
            send_sem=h_send.at[k, side],
            recv_sem=h_recv.at[k, side],
            device_id={"tm": right if side == 0 else left},
            device_id_type=MESH,
        )

    for k in range(2):
        for side in range(2):
            first_edge(k, side).start()

    def edge(step, side, g):
        where = (slice(None), slice(None), pl.ds(g * GROUP, GROUP), slice(None))
        return pltpu.make_async_remote_copy(
            src_ref=e_ref.at[(step, side) + where],
            dst_ref=h_ref.at[(2 + step, side) + where],
            send_sem=e_send.at[step, side, g],
            recv_sem=e_recv.at[step, side, g],
            device_id={"tm": right if side == 0 else left},
            device_id_type=MESH,
        )

    q = lax.broadcasted_iota(jnp.int32, (128, 128), 0)
    n = lax.broadcasted_iota(jnp.int32, (128, 128), 1)
    upper, diag = n >= q, n == q

    def build(sgn, lo, hi):
        def body(c, _):
            for part in range(2):
                def spread(i):
                    v = jnp.broadcast_to(taps_ref[c, pl.ds(i, 1), :], (128, 128))
                    return pltpu.roll(v, 0, 1, stride=1, stride_axis=0)

                neg = spread(sgn * 4 + part * 2)
                pos = spread(sgn * 4 + part * 2 + 1)
                last = taps_ref[c, pl.ds(8 + sgn * 2 + part, 1), :]
                blocks = (
                    jnp.where(upper, jnp.where(diag, last, 0.0), pos),
                    jnp.where(upper, pos, neg),
                    jnp.where(upper, neg, 0.0),
                )
                for b, t in enumerate(blocks):
                    big = t.astype(jnp.bfloat16)
                    small = (t - big.astype(jnp.float32)).astype(jnp.bfloat16)
                    t_hi[sgn, c, pl.ds(b * 128, 128), pl.ds(part * 128, 128)] = big
                    t_lo[sgn, c, pl.ds(b * 128, 128), pl.ds(part * 128, 128)] = small
            return 0

        lax.fori_loop(lo, hi, body, 0)

    def filtered(sgn, c, xs, halo):
        wide = []
        for part in range(2):
            for pol in range(2):
                v = xs[part * 2 + pol]
                before = halo[0, pol, part, pl.ds(c, 1), :]
                after = halo[1, pol, part, pl.ds(c, 1), :]
                wide.append(
                    jnp.concatenate(
                        [
                            jnp.where(row == 0, before, pltpu.roll(v, 1, 0)),
                            v,
                            jnp.where(row == 7, after, pltpu.roll(v, 7, 0)),
                        ],
                        axis=1,
                    )
                )
        win = jnp.concatenate(wide, axis=0)
        big = win.astype(jnp.bfloat16)
        small = (win - big.astype(jnp.float32)).astype(jnp.bfloat16)
        a = jnp.dot(
            jnp.concatenate([big, small], axis=0), t_hi[sgn, c], preferred_element_type=jnp.float32
        )
        b = jnp.dot(big, t_lo[sgn, c], preferred_element_type=jnp.float32)
        s = a[:32] + a[32:] + b
        re = s[:16, :128] - s[16:, 128:]
        im = s[:16, 128:] + s[16:, :128]
        return (re[:8], re[8:], im[:8], im[8:])

    def load(ref, c):
        return [ref[c, pl.ds(8 * i, 8), :] for i in range(4)]

    def store(ref, c, vs):
        for i in range(4):
            ref[c, pl.ds(8 * i, 8), :] = vs[i]

    def power(vs):
        return (vs[0] * vs[0] + vs[1] * vs[1]) + (vs[2] * vs[2] + vs[3] * vs[3])

    def turned(sign, vs, own, total):
        co, si = cos_sin((sign * GAMMA) * (2.0 * total - own))
        a, b, d, e = vs
        return (a * co - d * si, b * co - e * si, a * si + d * co, b * si + e * co)

    def run_filter(sgn, get, halo, step):
        total = jnp.zeros((8, 128), jnp.float32)
        for g in range(groups):
            def body(c, total):
                ys = filtered(sgn, c, get(c), halo)
                if step is None:
                    store(out_ref, c, ys)
                    return total
                own = power(ys)
                store(y_ref, c, ys)
                pw_ref[c] = own
                for part in range(2):
                    for pol in range(2):
                        v = ys[part * 2 + pol]
                        e_ref[step, 0, pol, part, pl.ds(c, 1), :] = v[7:8]
                        e_ref[step, 1, pol, part, pl.ds(c, 1), :] = v[0:1]
                return total + own

            total = lax.fori_loop(g * GROUP, (g + 1) * GROUP, body, total, unroll=4)
            if step is not None:
                edge(step, 0, g).start()
                edge(step, 1, g).start()
        return total

    def edges_arrived(step):
        for g in range(groups):
            for side in range(2):
                edge(step, side, g).wait()

    def chan_copy(k, d):
        return pltpu.make_async_remote_copy(
            src_ref=tsend.at[k],
            dst_ref=trecv.at[k, d - 1],
            send_sem=c_send.at[k, d - 1],
            recv_sem=c_recv.at[k, d - 1],
            device_id={"chan": lax.rem(ch + d, nc)},
            device_id_type=MESH,
        )

    def side_power(ref, side):
        out = None
        for pol in range(2):
            for part in range(2):
                v = ref[side, pol, part]
                out = v * v if out is None else out + v * v
        return out

    def exchange_total(k, total, halo, beside):
        tsend[k, pl.ds(0, 8), :] = total
        before = jnp.sum(side_power(halo, 0), axis=0, keepdims=True)
        after = jnp.sum(side_power(halo, 1), axis=0, keepdims=True)
        tsend[k, pl.ds(8, 8), :] = jnp.where(
            row == 0, before, jnp.where(row == 1, after, 0.0)
        )
        for d in range(1, nc):
            chan_copy(k, d).start()
        beside()
        whole = tsend[k]
        for d in range(1, nc):
            chan_copy(k, d).wait()
            whole = whole + trecv[k, d - 1]
        tot_ref[...] = whole

    def turn_halo(sign, halo):
        for side in range(2):
            own = side_power(halo, side)
            co, si = cos_sin(
                (sign * GAMMA) * (2.0 * tot_ref[pl.ds(8 + side, 1), :] - own)
            )
            for pol in range(2):
                a, b = halo[side, pol, 0], halo[side, pol, 1]
                hr_ref[side, pol, 0] = a * co - b * si
                hr_ref[side, pol, 1] = a * si + b * co

    build(0, 0, slots)
    for side in range(2):
        first_edge(0, side).wait()
    total = run_filter(0, lambda c: load(x_ref, c), h_ref.at[0], 0)

    edges_arrived(0)
    half = slots // 2
    exchange_total(0, total, h_ref.at[2], lambda: build(1, 0, half))
    turn_halo(1.0, h_ref.at[2])

    def forward_rotated(c):
        return turned(1.0, load(y_ref, c), pw_ref[c], tot_ref[pl.ds(0, 8), :])

    total = run_filter(0, forward_rotated, hr_ref, 1)
    edges_arrived(1)
    three = half + slots // 4
    exchange_total(1, total, h_ref.at[3], lambda: build(1, half, three))

    def sums(c, _):
        vs = forward_rotated(c)
        ns = load(noise_ref, c)
        store(z_ref, c, vs)
        cross = (vs[0] * ns[0] + vs[1] * ns[1]) + (vs[2] * ns[2] + vs[3] * ns[3])
        for i, v in enumerate((pw_ref[c], cross, power(ns))):
            stat[i, pl.ds(c, 1), :] = jnp.sum(v, axis=0, keepdims=True)
        return 0

    lax.fori_loop(0, slots, sums, 0, unroll=4)
    own_lane = lax.broadcasted_iota(jnp.int32, (slots, 128), 1) == lax.broadcasted_iota(
        jnp.int32, (slots, 128), 0
    )
    packed = jnp.zeros((8, 128), jnp.float32)
    for i in range(3):
        col = jnp.sum(stat[i], axis=1, keepdims=True)
        line = jnp.sum(jnp.where(own_lane, col, 0.0), axis=0, keepdims=True)
        packed = jnp.where(row == i, line, packed)
    ssend[...] = packed

    def stat_copy(d):
        return pltpu.make_async_remote_copy(
            src_ref=ssend,
            dst_ref=srecv.at[d - 1],
            send_sem=s_send.at[d - 1],
            recv_sem=s_recv.at[d - 1],
            device_id={"tm": lax.rem(tm + d, nt)},
            device_id_type=MESH,
        )

    def stat_start(d, _):
        stat_copy(d).start()
        return 0

    lax.fori_loop(1, nt, stat_start, 0)
    build(1, three, slots)
    turn_halo(1.0, h_ref.at[3])
    for side in range(2):
        first_edge(1, side).wait()

    def stat_add(d, acc):
        stat_copy(d).wait()
        return acc + srecv[d - 1]

    sums_all = lax.fori_loop(1, nt, stat_add, packed)
    field_sq, cross, noise_sq = sums_all[0:1], sums_all[1:2], sums_all[2:3]
    gain = lax.rsqrt(field_sq / total_len + EPS)
    arrival = (gain * gain * field_sq + 2.0 * gain * cross + noise_sq) / total_len
    rescale = jnp.sqrt(ATT ** (2 * STEPS) / (arrival + EPS))
    for i, v in enumerate((gain, rescale)):
        col = jnp.sum(jnp.where(own_lane, v, 0.0), axis=1, keepdims=True)
        gain_ref[i] = jnp.broadcast_to(col, (slots, 128))

    def amplify(c, total):
        g = gain_ref[0, pl.ds(c, 1), :]
        r = gain_ref[1, pl.ds(c, 1), :]
        vs, ns = load(z_ref, c), load(noise_ref, c)
        rec = [v * g + m for v, m in zip(vs, ns)]
        store(rec_ref, c, rec)
        back = [v * r for v in rec]
        store(y_ref, c, back)
        own = power(back)
        pw_ref[c] = own
        return total + own

    total = lax.fori_loop(0, slots, amplify, jnp.zeros((8, 128), jnp.float32), unroll=4)
    for side in range(2):
        for pol in range(2):
            for part in range(2):
                hr_ref[side, pol, part] = (
                    hr_ref[side, pol, part] * gain_ref[0] + h_ref[1, side, pol, part]
                ) * gain_ref[1]
    exchange_total(2, total, hr_ref, lambda: None)
    turn_halo(-1.0, hr_ref)

    def backward_rotated(c):
        return turned(-1.0, load(y_ref, c), pw_ref[c], tot_ref[pl.ds(0, 8), :])

    total = run_filter(1, backward_rotated, hr_ref, 2)
    edges_arrived(2)
    exchange_total(3, total, h_ref.at[4], lambda: None)
    turn_halo(-1.0, h_ref.at[4])
    run_filter(1, backward_rotated, hr_ref, None)


def on_device(field, noise, assign):
    nt, nc = lax.axis_size("tm"), lax.axis_size("chan")
    noise = noise[0]
    slots, length = field.shape[2], field.shape[3]
    blocks = length // REACH

    def arranged(a):
        a = a.reshape(2, 2, slots, blocks, REACH)
        return a.transpose(2, 1, 0, 3, 4).reshape(slots, 4 * blocks, REACH)

    def restored(a):
        a = a.reshape(slots, 2, 2, blocks, REACH)
        return a.transpose(2, 1, 0, 3, 4).reshape(2, 2, slots, length)

    f32, bf16 = jnp.float32, jnp.bfloat16
    vmem = pl.BlockSpec(memory_space=pltpu.VMEM)
    hbm = pl.BlockSpec(memory_space=pl.ANY)
    shape = jax.ShapeDtypeStruct((slots, 4 * blocks, REACH), f32)
    dma = pltpu.SemaphoreType.DMA
    received, recovered = pl.pallas_call(
        functools.partial(kernel, nt, nc, float(nt * length)),
        out_shape=(shape, shape),
        in_specs=[hbm, hbm, vmem, vmem, vmem],
        out_specs=(vmem, vmem),
        scratch_shapes=[
            pltpu.VMEM((2, slots, 3 * REACH, 2 * REACH), bf16),
            pltpu.VMEM((2, slots, 3 * REACH, 2 * REACH), bf16),
            pltpu.VMEM((slots, 4 * blocks, REACH), f32),
            pltpu.VMEM((slots, 4 * blocks, REACH), f32),
            pltpu.VMEM((slots, blocks, REACH), f32),
            pltpu.VMEM((5, 2, 2, 2, slots, REACH), f32),
            pltpu.VMEM((3, 2, 2, 2, slots, REACH), f32),
            pltpu.VMEM((2, 2, 2, slots, REACH), f32),
            pltpu.VMEM((4, 16, REACH), f32),
            pltpu.VMEM((4, nc - 1, 16, REACH), f32),
            pltpu.VMEM((16, REACH), f32),
            pltpu.VMEM((3, slots, REACH), f32),
            pltpu.VMEM((8, REACH), f32),
            pltpu.VMEM((nt - 1, 8, REACH), f32),
            pltpu.VMEM((2, slots, REACH), f32),
            dma((2, 2)),
            dma((2, 2)),
            dma((3, 2, slots // GROUP)),
            dma((3, 2, slots // GROUP)),
            dma((4, nc - 1)),
            dma((4, nc - 1)),
            dma((nt - 1,)),
            dma((nt - 1,)),
        ],
        compiler_params=pltpu.CompilerParams(
            collective_id=0, has_side_effects=True, vmem_limit_bytes=48 * 1024 * 1024
        ),
    )(field, noise, arranged(field), arranged(noise), tap_rows(assign))
    return restored(received), restored(recovered)


def solution(mesh):
    placed = (P(None, None, "chan", "tm"), P(None, None, None, "chan", "tm"), P("chan"))
    return jax.shard_map(
        on_device,
        mesh=mesh,
        in_specs=placed,
        out_specs=(P(None, None, "chan", "tm"), P(None, None, "chan", "tm")),
        check_vma=False,
    )
```

time: 541 us -> 58.1 us (0.11); the launches traced: 531 us -> 57.9 us
  matrix products: 433 us -> 0 us
  blocking collectives: 52.1 us -> 0 us
  Pallas kernels: 0 us -> 50.8 us
  starting transfers between devices: 24.2 us -> 0 us
  waiting for transfers between devices: 8.18 us -> 0 us
  other arithmetic: 7.78 us -> 0.67 us
    dot_general x16 -> x0, matrix products: 433 us -> none  [the longest x4 109 us: disperse(): jnp.einsum('pcjq,cqn->pcjn', real, mat_im, precision=high)]
    psum x5 -> x0, blocking collectives: 52.1 us -> none  [the longest x1 42.1 us: on_device(): field_sq, cross, noise_sq = lax.psum((field_sq, cross, noise_sq), 'tm')]
    pallas_call x0 -> x1, Pallas kernels: none -> 50.8 us  [on_device(): pl.pallas_call(functools.partial(kernel, nt, nc, float(nt * length)), out...]
    ppermute x8 -> x0, starting transfers between devices: 24.2 us -> none  [the longest x4 20.7 us: padded(): after = lax.ppermute(leading, axis, down)]
    ppermute x8 -> x0, waiting for transfers between devices: 8.18 us -> none  [the longest x4 8.17 us: padded(): before = lax.ppermute(last, axis, up)]
  transfers between devices with their start and end apart: 8 -> 0, of which waited for: 4 -> 0; matrix products, arithmetic and copies ran while one was open for 0% -> 0% of each run, Pallas kernels for 0% -> 0%
where the time goes in v1:
time: 58.1 us; the launch traced here: 57.9 us
  Pallas kernels  50.8 us (87%)
  local copies, waits for them, and re-layouts  5.65 us (10%)
  between operations  0.77 us (1%)
  other arithmetic  0.67 us (1%)
    pallas_call x1, Pallas kernels, on_device(): pl.pallas_call(functools.partial(kernel, nt, nc, float(nt * length)), out...  50.8 us
    reshape x4, local copies, waits for them, and re-layouts, restored(): return a.transpose(2, 1, 0, 3, 4).reshape(2, 2, slots, length)  2.74 us
    unnamed x8, local copies, waits for them, and re-layouts  1.85 us

profile of v1, /device:TPU:0, one launch (start us, length us, event | category | flops | bytes accessed | tf_op | source)
XLA Modules:
  0.0 57.9 jit_solution(18003012475240000452)
XLA Ops:
  0.6 0.0 copy-start.2
  0.6 0.6 %copy-done.2 = s32[32]{0:T(128)S(1)} copy-done((s32[32]{0:T(128)S(1)}, s32[32]{0:T(128)}, u32[]{:S(2)}) %copy-start.2) | copy-done | bytes 152
  1.3 0.2 exponential_reduce_fusion
  1.5 0.5 fusion.19
  2.0 0.0 copy-start.1
  2.0 0.1 slice_reduce_fusion
  2.1 0.1 slice_reduce_fusion.2
  2.2 0.1 stack_broadcast_in_dim.9
  2.3 0.1 stack_broadcast_in_dim.11
  2.4 0.1 stack_broadcast_in_dim.8
  2.5 0.1 stack_broadcast_in_dim.10
  2.7 0.3 stack.39.taps_ref
  3.0 0.0 copy-done.1
  3.0 0.1 copy.41
  3.1 0.0 copy-start
  3.1 0.1 copy.28
  3.2 1.0 %copy-done = f32[2,2,32,1024]{3,2,1,0:T(8,128)S(1)} copy-done((f32[2,2,32,1024]{3,2,1,0:T(8,128)S(1)}, f32[2,2,32,1024]{3,2,1,0:T(8,128)}, u32[]{:S(2)}) %copy-start) | copy-done | bytes 524312
  4.2 0.1 copy.40
  4.3 0.1 copy.27
  4.3 50.8 %shard_map.50 = (f32[32,32,128]{2,1,0:T(8,128)S(1)}, f32[32,32,128]{2,1,0:T(8,128)S(1)}) custom-call(f32[2,2,32,1024]{3,2,1,0:T(8,128)S(1)} %copy-done, f32[2,2,32,1024]{3,2,1,0:T(8,128)S(1)} %bitcast.55, f32[32,32,128]{2,1,0:T(8,128)S(1)} %bitcast.57, f32[32,32,128]{2,1,0:T(8,128)S(1)} %bitcast.56, f32[32,16,128]{2,1,0:T(8,128)S(1)} %stack.39.taps_ref), custom_call_target="tpu_custom_call" | custom-call | tf_op jit(solution)/shard_map/pallas_call | solution.py:384
  55.1 0.3 reshape.62
  55.4 1.1 %copy.38 = f32[2,2,32,1024]{3,2,1,0:T(8,128)} copy(f32[2,2,32,1024]{3,0,1,2:T(2,128)S(1)} %reshape.62) | data formatting | bytes 1048576 | tf_op jit(solution)/shard_map/reshape | solution.py:377
  56.5 0.3 reshape.63
  56.8 1.1 %copy.39 = f32[2,2,32,1024]{3,2,1,0:T(8,128)} copy(f32[2,2,32,1024]{3,0,1,2:T(2,128)S(1)} %reshape.63) | data formatting | bytes 1048576 | tf_op jit(solution)/shard_map/reshape | solution.py:377
  (8 shorter events, 0.1 us)
Async XLA Ops:
  0.6 0.7 %copy-start.2 = (s32[32]{0:T(128)S(1)}, s32[32]{0:T(128)}, u32[]{:S(2)}) copy-start(s32[32]{0:T(128)} %param.5) | copy-start | bytes 388
  2.0 1.0 %copy-start.1 = (f32[1,2,2,32,1024]{4,3,2,1,0:T(8,128)S(1)}, f32[1,2,2,32,1024]{4,3,2,1,0:T(8,128)}, u32[]{:S(2)}) copy-start(f32[1,2,2,32,1024]{4,3,2,1,0:T(8,128)} %param.4) | copy-start | bytes 1572868
  3.1 1.0 %copy-start = (f32[2,2,32,1024]{3,2,1,0:T(8,128)S(1)}, f32[2,2,32,1024]{3,2,1,0:T(8,128)}, u32[]{:S(2)}) copy-start(f32[2,2,32,1024]{3,2,1,0:T(8,128)} %field_hbm.1) | copy-start | bytes 1572868

commit v2 on v1

--- a/solution.py
+++ b/solution.py
@@ -61,7 +61,7 @@
     nt, nc, total_len,
     field_hbm, noise_hbm, x_ref, noise_ref, taps_ref,
     rec_ref, out_ref,
-    t_hi, t_lo, y_ref, z_ref, pw_ref, h_ref, e_ref, hr_ref, tsend, trecv, tot_ref, stat, ssend, srecv, gain_ref,
+    lhs_ref, t_hi, t_lo, y_ref, z_ref, pw_ref, h_ref, e_ref, hr_ref, tsend, trecv, tot_ref, stat, ssend, srecv, gain_ref,
     h_send, h_recv, e_send, e_recv, c_send, c_recv, s_send, s_recv,
 ):
     slots = x_ref.shape[0]
@@ -139,43 +139,14 @@
                     t_lo[sgn, c, pl.ds(b * 128, 128), pl.ds(part * 128, 128)] = small
             return 0
 
-        lax.fori_loop(lo, hi, body, 0)
-
-    def filtered(sgn, c, xs, halo):
-        wide = []
-        for part in range(2):
-            for pol in range(2):
-                v = xs[part * 2 + pol]
-                before = halo[0, pol, part, pl.ds(c, 1), :]
-                after = halo[1, pol, part, pl.ds(c, 1), :]
-                wide.append(
-                    jnp.concatenate(
-                        [
-                            jnp.where(row == 0, before, pltpu.roll(v, 1, 0)),
-                            v,
-                            jnp.where(row == 7, after, pltpu.roll(v, 7, 0)),
-                        ],
-                        axis=1,
-                    )
-                )
-        win = jnp.concatenate(wide, axis=0)
-        big = win.astype(jnp.bfloat16)
-        small = (win - big.astype(jnp.float32)).astype(jnp.bfloat16)
-        a = jnp.dot(
-            jnp.concatenate([big, small], axis=0), t_hi[sgn, c], preferred_element_type=jnp.float32
-        )
-        b = jnp.dot(big, t_lo[sgn, c], preferred_element_type=jnp.float32)
-        s = a[:32] + a[32:] + b
-        re = s[:16, :128] - s[16:, 128:]
-        im = s[:16, 128:] + s[16:, :128]
-        return (re[:8], re[8:], im[:8], im[8:])
-
-    def load(ref, c):
-        return [ref[c, pl.ds(8 * i, 8), :] for i in range(4)]
-
-    def store(ref, c, vs):
+        lax.fori_loop(lo, hi, body, 0, unroll=2)
+
+    def load(ref, c0):
+        return [ref[pl.ds(c0, GROUP), pl.ds(8 * i, 8), :] for i in range(4)]
+
+    def store(ref, c0, vs):
         for i in range(4):
-            ref[c, pl.ds(8 * i, 8), :] = vs[i]
+            ref[pl.ds(c0, GROUP), pl.ds(8 * i, 8), :] = vs[i]
 
     def power(vs):
         return (vs[0] * vs[0] + vs[1] * vs[1]) + (vs[2] * vs[2] + vs[3] * vs[3])
@@ -185,25 +156,60 @@
         a, b, d, e = vs
         return (a * co - d * si, b * co - e * si, a * si + d * co, b * si + e * co)
 
+    row3 = lax.broadcasted_iota(jnp.int32, (GROUP, 8, 128), 1)
+
+    def windows(buf, c0, xs, halo):
+        def spread(side, pol, part):
+            return jnp.stack(
+                [
+                    jnp.broadcast_to(halo[side, pol, part, pl.ds(c0 + i, 1), :], (8, 128))
+                    for i in range(GROUP)
+                ]
+            )
+
+        for part in range(2):
+            cuts = ([], [], [])
+            for pol in range(2):
+                v = xs[part * 2 + pol]
+                cuts[0].append(jnp.where(row3 == 0, spread(0, pol, part), pltpu.roll(v, 1, 1)))
+                cuts[1].append(v)
+                cuts[2].append(jnp.where(row3 == 7, spread(1, pol, part), pltpu.roll(v, 7, 1)))
+            for k in range(3):
+                win = jnp.concatenate(cuts[k], axis=1)
+                big = win.astype(jnp.bfloat16)
+                small = (win - big.astype(jnp.float32)).astype(jnp.bfloat16)
+                lhs_ref[buf, :, pl.ds(part * 16, 16), pl.ds(k * 128, 128)] = big
+                lhs_ref[buf, :, pl.ds(32 + part * 16, 16), pl.ds(k * 128, 128)] = small
+
     def run_filter(sgn, get, halo, step):
         total = jnp.zeros((8, 128), jnp.float32)
+        windows(0, 0, get(0), halo)
         for g in range(groups):
-            def body(c, total):
-                ys = filtered(sgn, c, get(c), halo)
+            if g + 1 < groups:
+                windows((g + 1) % 2, (g + 1) * GROUP, get((g + 1) * GROUP), halo)
+            for i in range(GROUP):
+                c = g * GROUP + i
+                lhs = lhs_ref[g % 2, i]
+                a = jnp.dot(lhs, t_hi[sgn, c], preferred_element_type=jnp.float32)
+                b = jnp.dot(lhs[:32], t_lo[sgn, c], preferred_element_type=jnp.float32)
+                s = a[:32] + a[32:] + b
+                re = s[:16, :128] - s[16:, 128:]
+                im = s[:16, 128:] + s[16:, :128]
                 if step is None:
-                    store(out_ref, c, ys)
-                    return total
+                    out_ref[c, pl.ds(0, 16), :] = re
+                    out_ref[c, pl.ds(16, 16), :] = im
+                    continue
+                ys = (re[:8], re[8:], im[:8], im[8:])
                 own = power(ys)
-                store(y_ref, c, ys)
+                total = total + own
+                y_ref[c, pl.ds(0, 16), :] = re
+                y_ref[c, pl.ds(16, 16), :] = im
                 pw_ref[c] = own
                 for part in range(2):
                     for pol in range(2):
                         v = ys[part * 2 + pol]
                         e_ref[step, 0, pol, part, pl.ds(c, 1), :] = v[7:8]
                         e_ref[step, 1, pol, part, pl.ds(c, 1), :] = v[0:1]
-                return total + own
-
-            total = lax.fori_loop(g * GROUP, (g + 1) * GROUP, body, total, unroll=4)
             if step is not None:
                 edge(step, 0, g).start()
                 edge(step, 1, g).start()
@@ -232,21 +238,38 @@
                 out = v * v if out is None else out + v * v
         return out
 
-    def exchange_total(k, total, halo, beside):
-        tsend[k, pl.ds(0, 8), :] = total
-        before = jnp.sum(side_power(halo, 0), axis=0, keepdims=True)
-        after = jnp.sum(side_power(halo, 1), axis=0, keepdims=True)
-        tsend[k, pl.ds(8, 8), :] = jnp.where(
-            row == 0, before, jnp.where(row == 1, after, 0.0)
-        )
+    def exchange_start(k, value):
+        tsend[k] = value
         for d in range(1, nc):
             chan_copy(k, d).start()
-        beside()
+
+    def exchange_end(k):
         whole = tsend[k]
         for d in range(1, nc):
             chan_copy(k, d).wait()
             whole = whole + trecv[k, d - 1]
-        tot_ref[...] = whole
+        tot_ref[pl.ds(8 * (k // 4), 8), :] = whole
+
+    def halo_total(halo):
+        before = jnp.sum(side_power(halo, 0), axis=0, keepdims=True)
+        after = jnp.sum(side_power(halo, 1), axis=0, keepdims=True)
+        return jnp.where(row == 0, before, jnp.where(row == 1, after, 0.0))
+
+    def halo_exchange(step, k):
+        edges_arrived(step)
+        exchange_start(4 + k, halo_total(h_ref.at[2 + step]))
+        exchange_end(4 + k)
+
+    def turn_all(rotated):
+        def body(g, _):
+            c0 = pl.multiple_of(g * GROUP, GROUP)
+            store(y_ref, c0, rotated(c0))
+            return 0
+
+        lax.fori_loop(0, groups, body, 0)
+
+    def kept(c0):
+        return load(y_ref, c0)
 
     def turn_halo(sign, halo):
         for side in range(2):
@@ -264,29 +287,34 @@
         first_edge(0, side).wait()
     total = run_filter(0, lambda c: load(x_ref, c), h_ref.at[0], 0)
 
-    edges_arrived(0)
     half = slots // 2
-    exchange_total(0, total, h_ref.at[2], lambda: build(1, 0, half))
+    exchange_start(0, total)
+    build(1, 0, half)
+    exchange_end(0)
+
+    def forward_rotated(c):
+        own = pw_ref[pl.ds(c, GROUP)]
+        return turned(1.0, load(y_ref, c), own, tot_ref[pl.ds(0, 8), :][None])
+
+    turn_all(forward_rotated)
+    halo_exchange(0, 0)
     turn_halo(1.0, h_ref.at[2])
 
-    def forward_rotated(c):
-        return turned(1.0, load(y_ref, c), pw_ref[c], tot_ref[pl.ds(0, 8), :])
-
-    total = run_filter(0, forward_rotated, hr_ref, 1)
-    edges_arrived(1)
-    three = half + slots // 4
-    exchange_total(1, total, h_ref.at[3], lambda: build(1, half, three))
-
-    def sums(c, _):
-        vs = forward_rotated(c)
-        ns = load(noise_ref, c)
-        store(z_ref, c, vs)
+    total = run_filter(0, kept, hr_ref, 1)
+    exchange_start(1, total)
+    exchange_end(1)
+
+    def sums(g, _):
+        c0 = pl.multiple_of(g * GROUP, GROUP)
+        vs = forward_rotated(c0)
+        ns = load(noise_ref, c0)
+        store(z_ref, c0, vs)
         cross = (vs[0] * ns[0] + vs[1] * ns[1]) + (vs[2] * ns[2] + vs[3] * ns[3])
-        for i, v in enumerate((pw_ref[c], cross, power(ns))):
-            stat[i, pl.ds(c, 1), :] = jnp.sum(v, axis=0, keepdims=True)
+        for i, v in enumerate((pw_ref[pl.ds(c0, GROUP)], cross, power(ns))):
+            stat[i, pl.ds(c0, GROUP), :] = jnp.sum(v, axis=1)
         return 0
 
-    lax.fori_loop(0, slots, sums, 0, unroll=4)
+    lax.fori_loop(0, groups, sums, 0)
     own_lane = lax.broadcasted_iota(jnp.int32, (slots, 128), 1) == lax.broadcasted_iota(
         jnp.int32, (slots, 128), 0
     )
@@ -312,7 +340,8 @@
         return 0
 
     lax.fori_loop(1, nt, stat_start, 0)
-    build(1, three, slots)
+    build(1, half, slots)
+    halo_exchange(1, 1)
     turn_halo(1.0, h_ref.at[3])
     for side in range(2):
         first_edge(1, side).wait()
@@ -330,36 +359,51 @@
         col = jnp.sum(jnp.where(own_lane, v, 0.0), axis=1, keepdims=True)
         gain_ref[i] = jnp.broadcast_to(col, (slots, 128))
 
-    def amplify(c, total):
-        g = gain_ref[0, pl.ds(c, 1), :]
-        r = gain_ref[1, pl.ds(c, 1), :]
-        vs, ns = load(z_ref, c), load(noise_ref, c)
+    def amplify(k, total):
+        c0 = pl.multiple_of(k * GROUP, GROUP)
+
+        def spread(i):
+            return jnp.stack(
+                [
+                    jnp.broadcast_to(gain_ref[i, pl.ds(c0 + j, 1), :], (8, 128))
+                    for j in range(GROUP)
+                ]
+            )
+
+        g, r = spread(0), spread(1)
+        vs, ns = load(z_ref, c0), load(noise_ref, c0)
         rec = [v * g + m for v, m in zip(vs, ns)]
-        store(rec_ref, c, rec)
+        store(rec_ref, c0, rec)
         back = [v * r for v in rec]
-        store(y_ref, c, back)
+        store(y_ref, c0, back)
         own = power(back)
-        pw_ref[c] = own
-        return total + own
-
-    total = lax.fori_loop(0, slots, amplify, jnp.zeros((8, 128), jnp.float32), unroll=4)
+        pw_ref[pl.ds(c0, GROUP)] = own
+        return total + jnp.sum(own, axis=0)
+
+    total = lax.fori_loop(0, groups, amplify, jnp.zeros((8, 128), jnp.float32))
     for side in range(2):
         for pol in range(2):
             for part in range(2):
                 hr_ref[side, pol, part] = (
                     hr_ref[side, pol, part] * gain_ref[0] + h_ref[1, side, pol, part]
                 ) * gain_ref[1]
-    exchange_total(2, total, hr_ref, lambda: None)
+    exchange_start(2, total)
+    exchange_start(6, halo_total(hr_ref))
+    exchange_end(2)
+    exchange_end(6)
     turn_halo(-1.0, hr_ref)
 
     def backward_rotated(c):
-        return turned(-1.0, load(y_ref, c), pw_ref[c], tot_ref[pl.ds(0, 8), :])
+        own = pw_ref[pl.ds(c, GROUP)]
+        return turned(-1.0, load(y_ref, c), own, tot_ref[pl.ds(0, 8), :][None])
 
     total = run_filter(1, backward_rotated, hr_ref, 2)
-    edges_arrived(2)
-    exchange_total(3, total, h_ref.at[4], lambda: None)
+    exchange_start(3, total)
+    exchange_end(3)
+    turn_all(backward_rotated)
+    halo_exchange(2, 3)
     turn_halo(-1.0, h_ref.at[4])
-    run_filter(1, backward_rotated, hr_ref, None)
+    run_filter(1, kept, hr_ref, None)
 
 
 def on_device(field, noise, assign):
@@ -387,6 +431,7 @@
         in_specs=[hbm, hbm, vmem, vmem, vmem],
         out_specs=(vmem, vmem),
         scratch_shapes=[
+            pltpu.VMEM((2, GROUP, 64, 3 * REACH), bf16),
             pltpu.VMEM((2, slots, 3 * REACH, 2 * REACH), bf16),
             pltpu.VMEM((2, slots, 3 * REACH, 2 * REACH), bf16),
             pltpu.VMEM((slots, 4 * blocks, REACH), f32),
@@ -395,8 +440,8 @@
             pltpu.VMEM((5, 2, 2, 2, slots, REACH), f32),
             pltpu.VMEM((3, 2, 2, 2, slots, REACH), f32),
             pltpu.VMEM((2, 2, 2, slots, REACH), f32),
-            pltpu.VMEM((4, 16, REACH), f32),
-            pltpu.VMEM((4, nc - 1, 16, REACH), f32),
+            pltpu.VMEM((8, 8, REACH), f32),
+            pltpu.VMEM((8, nc - 1, 8, REACH), f32),
             pltpu.VMEM((16, REACH), f32),
             pltpu.VMEM((3, slots, REACH), f32),
             pltpu.VMEM((8, REACH), f32),
@@ -406,8 +451,8 @@
             dma((2, 2)),
             dma((3, 2, slots // GROUP)),
             dma((3, 2, slots // GROUP)),
-            dma((4, nc - 1)),
-            dma((4, nc - 1)),
+            dma((8, nc - 1)),
+            dma((8, nc - 1)),
             dma((nt - 1,)),
             dma((nt - 1,)),
         ],

time: 58.1 us -> 49.8 us (0.86)
  Pallas kernels: 50.8 us -> 42.5 us
    pallas_call x1, Pallas kernels: 50.8 us -> 42.5 us  [on_device(): pl.pallas_call(functools.partial(kernel, nt, nc, float(nt * length)), out...]
where the time goes in v2:
time: 49.8 us; the launch traced here: 49.6 us
  Pallas kernels  42.5 us (85%)
  local copies, waits for them, and re-layouts  5.65 us (11%)
  between operations  0.77 us (2%)
  other arithmetic  0.67 us (1%)
    pallas_call x1, Pallas kernels, on_device(): pl.pallas_call(functools.partial(kernel, nt, nc, float(nt * length)), out...  42.5 us
    reshape x4, local copies, waits for them, and re-layouts, restored(): return a.transpose(2, 1, 0, 3, 4).reshape(2, 2, slots, length)  2.74 us
    unnamed x8, local copies, waits for them, and re-layouts  1.85 us

profile of v2, /device:TPU:0, one launch (start us, length us, event | category | flops | bytes accessed | tf_op | source)
XLA Modules:
  0.0 49.6 jit_solution(18040753691333357193)
XLA Ops:
  0.6 0.0 copy-start.2
  0.6 0.6 %copy-done.2 = s32[32]{0:T(128)S(1)} copy-done((s32[32]{0:T(128)S(1)}, s32[32]{0:T(128)}, u32[]{:S(2)}) %copy-start.2) | copy-done | bytes 152
  1.3 0.2 exponential_reduce_fusion
  1.5 0.5 fusion.19
  2.0 0.0 copy-start.1
  2.0 0.1 slice_reduce_fusion
  2.1 0.1 slice_reduce_fusion.2
  2.2 0.1 stack_broadcast_in_dim.9
  2.3 0.1 stack_broadcast_in_dim.11
  2.4 0.1 stack_broadcast_in_dim.8
  2.5 0.1 stack_broadcast_in_dim.10
  2.7 0.3 stack.39.taps_ref
  3.0 0.0 copy-done.1
  3.0 0.1 copy.41
  3.1 0.0 copy-start
  3.1 0.1 copy.28
  3.2 1.0 %copy-done = f32[2,2,32,1024]{3,2,1,0:T(8,128)S(1)} copy-done((f32[2,2,32,1024]{3,2,1,0:T(8,128)S(1)}, f32[2,2,32,1024]{3,2,1,0:T(8,128)}, u32[]{:S(2)}) %copy-start) | copy-done | bytes 524312
  4.2 0.1 copy.40
  4.3 0.1 copy.27
  4.3 42.5 %shard_map.50 = (f32[32,32,128]{2,1,0:T(8,128)S(1)}, f32[32,32,128]{2,1,0:T(8,128)S(1)}) custom-call(f32[2,2,32,1024]{3,2,1,0:T(8,128)S(1)} %copy-done, f32[2,2,32,1024]{3,2,1,0:T(8,128)S(1)} %bitcast.55, f32[32,32,128]{2,1,0:T(8,128)S(1)} %bitcast.57, f32[32,32,128]{2,1,0:T(8,128)S(1)} %bitcast.56, f32[32,16,128]{2,1,0:T(8,128)S(1)} %stack.39.taps_ref), custom_call_target="tpu_custom_call" | custom-call | tf_op jit(solution)/shard_map/pallas_call | solution.py:428
  46.9 0.3 reshape.62
  47.1 1.1 %copy.38 = f32[2,2,32,1024]{3,2,1,0:T(8,128)} copy(f32[2,2,32,1024]{3,0,1,2:T(2,128)S(1)} %reshape.62) | data formatting | bytes 1048576 | tf_op jit(solution)/shard_map/reshape | solution.py:421
  48.2 0.3 reshape.63
  48.5 1.1 %copy.39 = f32[2,2,32,1024]{3,2,1,0:T(8,128)} copy(f32[2,2,32,1024]{3,0,1,2:T(2,128)S(1)} %reshape.63) | data formatting | bytes 1048576 | tf_op jit(solution)/shard_map/reshape | solution.py:421
  (8 shorter events, 0.1 us)
Async XLA Ops:
  0.6 0.7 %copy-start.2 = (s32[32]{0:T(128)S(1)}, s32[32]{0:T(128)}, u32[]{:S(2)}) copy-start(s32[32]{0:T(128)} %param.5) | copy-start | bytes 388
  2.0 1.0 %copy-start.1 = (f32[1,2,2,32,1024]{4,3,2,1,0:T(8,128)S(1)}, f32[1,2,2,32,1024]{4,3,2,1,0:T(8,128)}, u32[]{:S(2)}) copy-start(f32[1,2,2,32,1024]{4,3,2,1,0:T(8,128)} %param.4) | copy-start | bytes 1572868
  3.1 1.0 %copy-start = (f32[2,2,32,1024]{3,2,1,0:T(8,128)S(1)}, f32[2,2,32,1024]{3,2,1,0:T(8,128)}, u32[]{:S(2)}) copy-start(f32[2,2,32,1024]{3,2,1,0:T(8,128)} %field_hbm.1) | copy-start | bytes 1572868
